TPU v7x, 256 devices: a whole 4x4x8 slice. The times are simulated.
256 devices in a mesh: ep: 64 (over y, z, core), dp: 4 (over x).
Axes of the slice: x: 4, y: 4, z: 8, core: 2. Of those that a mesh axis runs over, the one named last changes fastest.
Arguments:
- tokens: bfloat16 [32768, 2048], P(('dp', 'ep')), parts along dimension 0, may hold values from -6 to 6
- routes: int32 [32768, 10], P(('dp', 'ep')), parts along dimension 0, may hold values from 0 to 63, all different within a row; in each aligned block of 128 rows (0 to 127, 128 to 255, ...) at most 24 rows name the same one
- gate_share: float32 [32768, 10], P(('dp', 'ep')), parts along dimension 0, may hold values from 0.1 to 1
- norm_gain: float32 [2048], replicated, may hold values from 0.1 to 1.9
- w_gate: bfloat16 [64, 2048, 512], P('ep'), may hold values from -0.125 to 0.125
- w_up: bfloat16 [64, 2048, 512], P('ep'), may hold values from -0.125 to 0.125
- w_down: bfloat16 [64, 512, 2048], P('ep'), may hold values from -0.25 to 0.25
- shared_gate: bfloat16 [2048, 256], replicated, may hold values from -0.125 to 0.125
- shared_up: bfloat16 [2048, 256], replicated, may hold values from -0.125 to 0.125
- shared_down: bfloat16 [256, 2048], replicated, may hold values from -0.375 to 0.375
- shared_switch: bfloat16 [2048], replicated, may hold values from -0.125 to 0.125
- post_gain: float32 [2048], replicated, may hold values from 0.1 to 1.9
- value_w: bfloat16 [2048, 2048], P('ep'), may hold values from -0.125 to 0.125
- conv_w: float32 [4, 2048], replicated, may hold values from -3 to 3
Outputs:
- expert_mix: bfloat16 [32768, 2048], P(('dp', 'ep')), parts along dimension 0
- value_conv: bfloat16 [32768, 2048], P(('dp', 'ep')), parts along dimension 0
There are 4 independent parts, one for each index of `dp`. A program takes and returns all parts, laid end to end along the dimension named above; an argument that names none is the same for every part. Nothing has to cross between parts.
Inputs may be any that keep to these rules, and one draw needn't show every extreme that they name: `routes`: each row names 10 different experts. Among the 128 rows of one device no expert is named more than 24 times, a bound that some block reaches.
All inputs are finite; a program needn't handle non-finite values.
Results may differ from a plain program's by a relative error of at most 0.0067.
Values may be sent and summed in bfloat16 or wider, within the bound.
A program may use at most 128 MiB of HBM per device.

v0:
```python
import jax
import jax.numpy as jnp
from jax import lax
from jax.sharding import PartitionSpec as P

CAP = 24


def shifted(block, axis, distance):
    devices = range(lax.axis_size(axis))
    route = [(i - distance, i) for i in devices if i - distance in devices]
    return lax.ppermute(block, axis, route)


def rms_norm(values, gain):
    return values * lax.rsqrt(jnp.mean(values * values, axis=-1, keepdims=True) + 1e-06) * gain


def run_experts(received, w_gate, w_up, w_down):
    local_count = w_gate.shape[0]
    blocked = received.reshape(-1, local_count, received.shape[1], received.shape[2])
    gate_act = jnp.einsum("secd,edf->secf", blocked, w_gate, preferred_element_type=jnp.float32)
    up_act = jnp.einsum("secd,edf->secf", blocked, w_up, preferred_element_type=jnp.float32)
    hidden = (jax.nn.silu(gate_act) * up_act).astype(jnp.bfloat16)
    output = jnp.einsum(
        "secf,efd->secd", hidden, w_down, preferred_element_type=jnp.float32
    ).astype(jnp.bfloat16)
    return output.reshape(received.shape)


def project_values(left_rows, value_w):
    projected = jnp.dot(
        left_rows,
        lax.all_gather(value_w, "ep", axis=0, tiled=True),
        preferred_element_type=jnp.float32,
    )
    return projected.astype(jnp.bfloat16)


def local(
    tokens,
    routes,
    gate_share,
    norm_gain,
    w_gate,
    w_up,
    w_down,
    shared_gate,
    shared_up,
    shared_down,
    shared_switch,
    post_gain,
    value_w,
    conv_w,
):
    tok_rows, width = tokens.shape
    top_count = routes.shape[1]
    experts_all = w_gate.shape[0] * lax.axis_size("ep")
    slots = CAP
    channels = value_w.shape[1]
    taps = conv_w.shape[0]
    resid = tokens.astype(jnp.float32)
    normed = rms_norm(resid, norm_gain).astype(jnp.bfloat16)
    shares = gate_share / jnp.sum(gate_share, axis=-1, keepdims=True)
    entries = routes.reshape(-1)
    onehot = (entries[:, None] == jnp.arange(experts_all, dtype=jnp.int32)[None, :]).astype(
        jnp.int32
    )
    slot_rank = jnp.sum((jnp.cumsum(onehot, axis=0) - onehot) * onehot, axis=-1)
    target = entries * slots + slot_rank
    owner_rows = jnp.arange(tok_rows * top_count, dtype=jnp.int32) // top_count
    sender_rows = jnp.zeros((experts_all * slots,), jnp.int32).at[target].set(owner_rows)
    filled = (
        jnp.zeros((experts_all * slots,), jnp.bfloat16)
        .at[target]
        .set(jnp.ones((tok_rows * top_count,), jnp.bfloat16))
    )
    outgoing = (normed[sender_rows] * filled[:, None]).reshape(experts_all, slots, width)
    received = lax.all_to_all(outgoing, "ep", split_axis=0, concat_axis=0, tiled=True)
    computed = run_experts(received, w_gate, w_up, w_down)
    returned = lax.all_to_all(computed, "ep", split_axis=0, concat_axis=0, tiled=True)
    picked = returned.reshape(experts_all * slots, width)[target].astype(jnp.float32)
    routed = jnp.sum(
        (picked * shares.reshape(-1)[:, None]).reshape(tok_rows, top_count, width), axis=1
    )
    shared_hidden = (
        jax.nn.silu(jnp.dot(normed, shared_gate, preferred_element_type=jnp.float32))
        * jnp.dot(normed, shared_up, preferred_element_type=jnp.float32)
    ).astype(jnp.bfloat16)
    switch = jax.nn.sigmoid(
        jnp.dot(normed, shared_switch.reshape(width, 1), preferred_element_type=jnp.float32)
    )
    mixture = routed + switch * jnp.dot(
        shared_hidden, shared_down, preferred_element_type=jnp.float32
    )
    expert_mix = mixture.astype(jnp.bfloat16)
    post_normed = rms_norm(resid + mixture, post_gain).astype(jnp.bfloat16)
    values = project_values(post_normed, value_w)
    previous = shifted(values[tok_rows - (taps - 1) :], "ep", 1)
    extended = jnp.concatenate([previous, values], axis=0)
    widened = extended.astype(jnp.float32)
    summed = jnp.zeros((tok_rows, channels), jnp.float32)
    for tap_index in range(taps):
        summed = summed + conv_w[tap_index][None, :] * widened[tap_index : tap_index + tok_rows]
    value_conv = jax.nn.silu(summed).astype(jnp.bfloat16)
    return (expert_mix, value_conv)


def solution(mesh):
    placed = (
        P(("dp", "ep"), None),
        P(("dp", "ep"), None),
        P(("dp", "ep"), None),
        P(),
        P("ep", None, None),
        P("ep", None, None),
        P("ep", None, None),
        P(),
        P(),
        P(),
        P(),
        P(),
        P("ep", None),
        P(),
    )
    return jax.shard_map(
        local,
        mesh=mesh,
        in_specs=placed,
        out_specs=(P(("dp", "ep"), None), P(("dp", "ep"), None)),
        check_vma=False,
    )
```

profile of v0, /device:TPU:6, one launch (start us, length us, event | category | flops | bytes accessed | tf_op | source)
XLA Modules:
  0.0 477.0 jit_solution(15682650447852429042)
XLA Ops:
  7.2 1.0 copy.18
  8.4 0.7 broadcast_multiply_fusion.1
  9.1 0.8 fusion.30
  10.0 31.5 %reduce-window.6 = s32[64,10,128]{2,1,0:T(8,128)S(1)} reduce-window(s32[64,10,128]{2,1,0:T(8,128)} %fusion.30, s32[]{:T(128)} %constant.16.clone.1), window={size=1x1x128 pad=0_0x0_0x127_0}, to_apply=%region_1.0 | reduce-window | flops 10403840 | bytes 655364 | tf_op jit(solution)/shard_map/reduce-window
  41.5 1.0 slice.48
  42.5 1.3 copy.20
  43.9 1.0 broadcast_add_fusion
  45.1 1.2 fusion.33
  46.4 5.2 %scatter_custom_fusion = s32[1536]{0:T(1024)S(1)} fusion(s32[1280]{0:T(1024)S(1)} %fusion.43, s32[1280]{0:T(1024)S(1)} %add_select_fusion, s32[]{:T(128)} %constant.16.clone.1), kind=kCustom, calls=%fused_computation.77 | custom fusion | bytes 6148 | tf_op jit(solution)/shard_map/scatter | solution.py:72
  51.7 0.2 fusion.18
  51.9 12.6 %scatter_custom_fusion.1 = bf16[1536]{0:T(1024)(128)(2,1)S(1)} fusion(s32[1280]{0:T(1024)S(1)} %fusion.43, bf16[1280]{0:T(1024)(128)(2,1)S(1)} %broadcast.106, bf16[]{:T(256)} %constant.41.clone.1), kind=kCustom, calls=%fused_computation.79 | custom fusion | bytes 3074 | tf_op jit(solution)/shard_map/scatter | solution.py:76
  64.6 0.2 fusion.20
  64.8 7.1 %gather_fusion = bf16[1536,2048]{1,0:T(8,128)(2,1)} fusion(bf16[128,2048]{1,0:T(8,128)(2,1)S(1)} %fusion.20, s32[2048]{0:T(1024)S(1)} %pad_clamp_fusion.1), kind=kCustom, calls=%fused_computation | custom fusion | bytes 12589056 | tf_op jit(solution)/shard_map/gather | solution.py:78
  71.9 5.9 %broadcast_multiply_fusion = bf16[64,24,2048]{2,1,0:T(8,128)(2,1)} fusion(bf16[64,24,2048]{2,1,0:T(8,128)(2,1)} %bitcast.99, bf16[64,24]{1,0:T(8,128)(2,1)S(1)} %mul.152), kind=kLoop, calls=%fused_computation.13 | loop fusion | flops 3145728 | bytes 12585984 | tf_op jit(solution)/shard_map/mul | solution.py:78
  77.8 12.3 %all-to-all-start = ((bf16[64,24,2048]{2,1,0:T(8,128)(2,1)}), bf16[64,24,2048]{2,1,0:T(8,128)(2,1)}, u32[]{:S(2)}, u32[]{:S(2)}) async-start(bf16[64,24,2048]{2,1,0:T(8,128)(2,1)} %broadcast_multiply_fusion), calls=%async_computation | async-start | bytes 12582912 | tf_op jit(solution)/shard_map/all_to_all | solution.py:79
  90.2 0.2 all-gather.2.cloned.1.call-start
  90.4 0.5 all-gather.2.cloned.1.call-update
  90.9 164.1 %all-to-all-done = bf16[64,24,2048]{2,1,0:T(8,128)(2,1)} async-done(((bf16[64,24,2048]{2,1,0:T(8,128)(2,1)}), bf16[64,24,2048]{2,1,0:T(8,128)(2,1)}, u32[]{:S(2)}, u32[]{:S(2)}) %all-to-all-start) | async-done | bytes 6291488 | tf_op jit(solution)/shard_map/all_to_all | solution.py:79
  255.0 8.5 %fusion.10 = f32[64,24,512]{2,1,0:T(8,128)} fusion(bf16[64,24,2048]{2,1,0:T(8,128)(2,1)} %all-to-all-done, bf16[1,2048,512]{2,1,0:T(8,128)(2,1)} %param.18), kind=kOutput, calls=%fused_computation.20 | convolution fusion | flops 3221225472 | bytes 11534336 | tf_op jit(solution)/shard_map/secd,edf->secf/dot_general | solution.py:22
  263.6 11.8 %convolution_convert_fusion = bf16[64,24,2048]{2,1,0:T(8,128)(2,1)} fusion(bf16[1,512,2048]{2,1,0:T(8,128)(2,1)S(1)} %copy-done, f32[64,24,512]{2,1,0:T(8,128)} %fusion.10, bf16[64,24,2048]{2,1,0:T(8,128)(2,1)} %all-to-all-done, bf16[1,2048,512]{2,1,0:T(8,128)(2,1)} %param.19), kind=kOutput, calls=%fused_computation.5 | convolution fusion | flops 6450315264 | bytes 19922944 | tf_op jit(solution)/shard_map/secf,efd->secd/dot_general | solution.py:25
  275.4 6.9 %all-to-all-start.1 = ((bf16[64,24,2048]{2,1,0:T(8,128)(2,1)}), bf16[64,24,2048]{2,1,0:T(8,128)(2,1)}, u32[]{:S(2)}, u32[]{:S(2)}) async-start(bf16[64,24,2048]{2,1,0:T(8,128)(2,1)} %convolution_convert_fusion), calls=%async_computation.1 | async-start | bytes 12582912 | tf_op jit(solution)/shard_map/all_to_all | solution.py:81
  282.5 0.2 fusion.17
  282.7 0.3 fusion.51
  283.1 139.3 %all-to-all-done.1 = bf16[64,24,2048]{2,1,0:T(8,128)(2,1)} async-done(((bf16[64,24,2048]{2,1,0:T(8,128)(2,1)}), bf16[64,24,2048]{2,1,0:T(8,128)(2,1)}, u32[]{:S(2)}, u32[]{:S(2)}) %all-to-all-start.1) | async-done | bytes 6291488 | tf_op jit(solution)/shard_map/all_to_all | solution.py:81
  422.3 14.5 %gather_fusion.1 = bf16[1280,2048]{1,0:T(8,128)(2,1)} fusion(bf16[1536,2048]{1,0:T(8,128)(2,1)} %bitcast.18, s32[2048]{0:T(1024)S(1)} %pad_clamp_fusion), kind=kCustom, calls=%fused_computation.1 | custom fusion | bytes 10490880 | tf_op jit(solution)/shard_map/gather | solution.py:82
  436.8 10.4 %reshape.127 = f32[128,10,2048]{2,1,0:T(8,128)} reshape(bf16[1280,2048]{1,0:T(8,128)(2,1)} %gather_fusion.1) | data formatting | bytes 15728640 | tf_op jit(solution)/shard_map/convert_element_type | solution.py:82
  447.2 9.6 %multiply_reduce_fusion = f32[128,2048]{1,0:T(8,128)S(1)} fusion(f32[128,10,2048]{2,1,0:T(8,128)} %reshape.127, f32[128,10]{1,0:T(8,128)S(1)} %copy.22), kind=kLoop, calls=%fused_computation.4 | loop fusion | flops 4980736 | bytes 11539456 | tf_op jit(solution)/shard_map/reduce_sum | solution.py:83
  456.9 3.2 multiply_reduce_fusion.1
  460.0 5.1 %convolution_convert_fusion.1 = bf16[128,2048]{1,0:T(8,128)(2,1)S(1)} fusion(bf16[2048,2048]{1,0:T(8,128)(2,1)} %all-gather.2.cloned.1.call-done, f32[128,2048]{1,0:T(8,128)} %get-tuple-element.8, bf16[128,2048]{1,0:T(8,128)(2,1)S(1)} %copy-done.2, f32[2048]{0:T(1024)S(1)} %copy-done.5, f32[128]{0:T(128)S(1)} %add_rsqrt_fusion), kind=kOutput, calls=%fused_computation.16 | convolution fusion | flops 1075314688 | bytes 10494464 | tf_op jit(solution)/shard_map/dot_general | solution.py:32
  465.2 2.5 collective-permute-start
  467.7 0.8 collective-permute-done
  468.7 1.4 multiply_convert_fusion
  (43 shorter events, 1.2 us)
Async XLA Ops:
  7.2 256.4 %copy-start = (bf16[1,512,2048]{2,1,0:T(8,128)(2,1)S(1)}, bf16[1,512,2048]{2,1,0:T(8,128)(2,1)}, u32[]{:S(2)}) copy-start(bf16[1,512,2048]{2,1,0:T(8,128)(2,1)} %param.20) | copy-start | bytes 6291460
  7.2 44.5 %copy-start.2 = (bf16[128,2048]{1,0:T(8,128)(2,1)S(1)}, bf16[128,2048]{1,0:T(8,128)(2,1)}, u32[]{:S(2)}) copy-start(bf16[128,2048]{1,0:T(8,128)(2,1)} %param.14) | copy-start | bytes 1572868
  7.2 57.4 %copy-start.8 = (f32[2048]{0:T(1024)S(1)}, f32[2048]{0:T(1024)}, u32[]{:S(2)}) copy-start(f32[2048]{0:T(1024)} %param.17) | copy-start | bytes 24580
  77.8 177.2 %all-to-all-start = ((bf16[64,24,2048]{2,1,0:T(8,128)(2,1)}), bf16[64,24,2048]{2,1,0:T(8,128)(2,1)}, u32[]{:S(2)}, u32[]{:S(2)}) async-start(bf16[64,24,2048]{2,1,0:T(8,128)(2,1)} %broadcast_multiply_fusion), calls=%async_computation | async-start | bytes 12582912 | tf_op jit(solution)/shard_map/all_to_all | solution.py:79
  90.2 369.8 %all-gather.2.cloned.1.call-start = ((), (), s32[]{:S(2)}) async-start(), calls=%async_computation.2 | async-start | bytes 8519680 | tf_op jit(solution)/shard_map/all_gather | solution.py:34
  275.4 6.9 %copy-start.7 = (f32[128,10]{0,1:T(8,128)S(1)}, f32[128,10]{0,1:T(8,128)}, u32[]{:S(2)}) copy-start(f32[128,10]{0,1:T(8,128)} %param.16) | copy-start | bytes 15364
  275.4 7.1 %copy-start.9 = (bf16[2048]{0:T(1024)(128)(2,1)S(1)}, bf16[2048]{0:T(1024)(128)(2,1)}, u32[]{:S(2)}) copy-start(bf16[2048]{0:T(1024)(128)(2,1)} %param.24) | copy-start | bytes 12292
  275.4 7.4 %copy-start.4 = (bf16[2048,256]{1,0:T(8,128)(2,1)S(1)}, bf16[2048,256]{1,0:T(8,128)(2,1)}, u32[]{:S(2)}) copy-start(bf16[2048,256]{1,0:T(8,128)(2,1)} %param.21) | copy-start | bytes 3145732
  275.4 147.0 %all-to-all-start.1 = ((bf16[64,24,2048]{2,1,0:T(8,128)(2,1)}), bf16[64,24,2048]{2,1,0:T(8,128)(2,1)}, u32[]{:S(2)}, u32[]{:S(2)}) async-start(bf16[64,24,2048]{2,1,0:T(8,128)(2,1)} %convolution_convert_fusion), calls=%async_computation.1 | async-start | bytes 12582912 | tf_op jit(solution)/shard_map/all_to_all | solution.py:81
  447.2 9.6 %copy-start.3 = (bf16[256,2048]{1,0:T(8,128)(2,1)S(1)}, bf16[256,2048]{1,0:T(8,128)(2,1)}, u32[]{:S(2)}) copy-start(bf16[256,2048]{1,0:T(8,128)(2,1)} %param.23) | copy-start | bytes 3145732
  456.8 3.2 copy-start.5
  460.0 7.7 %copy-start.6 = (f32[4,2048]{1,0:T(4,128)S(1)}, f32[4,2048]{1,0:T(4,128)}, u32[]{:S(2)}) copy-start(f32[4,2048]{1,0:T(4,128)} %param.27) | copy-start | bytes 98308
  460.0 10.1 %copy-start.1 = (bf16[1,512,2048]{2,1,0:T(8,128)(2,1)S(1)}, bf16[1,512,2048]{2,1,0:T(8,128)(2,1)}, u32[]{:S(2)}) copy-start(bf16[1,512,2048]{2,1,0:T(8,128)(2,1)} %param.20) | copy-start | bytes 6291460
  465.2 3.3 collective-permute-start
Sparse Core Ops, SparseCore 0:
  93.8 133.9 all-gather.1
where the time goes:
time: 483 us; the launch traced here: 477 us
  waiting for transfers between devices  305 us (63%)
  local copies, waits for them, and re-layouts  54 us (11%)
  other arithmetic  52.8 us (11%)
  matrix products  29.2 us (6%)
  starting transfers between devices  21.9 us (5%)
  between operations  14.3 us (3%)
    all_to_all x1, waiting for transfers between devices, local(): lax.all_to_all(outgoing, 'ep', split_axis=0, concat_axis=0, tiled=True)  164 us
    all_to_all x1, waiting for transfers between devices, local(): lax.all_to_all(computed, 'ep', split_axis=0, concat_axis=0, tiled=True)  139 us
    another operation x3, other arithmetic  32.5 us
    gather x1, local copies, waits for them, and re-layouts, local(): returned.reshape(experts_all * slots, width)[target].astype(jnp.float32)  14.5 us
    scatter x1, local copies, waits for them, and re-layouts, local(): filled = jnp.zeros((experts_all * slots,), jnp.bfloat16).at[target].set(j...  12.6 us
    all_to_all x1, starting transfers between devices, local(): lax.all_to_all(outgoing, 'ep', split_axis=0, concat_axis=0, tiled=True)  12.3 us
    dot_general x1, matrix products, run_experts(): jnp.einsum('secf,efd->secd', hidden, w_down, preferred_element_type=jnp.f...  11.8 us
    convert_element_type x1, local copies, waits for them, and re-layouts, local(): returned.reshape(experts_all * slots, width)[target].astype(jnp.float32)  10.4 us
  transfers between devices with their start and end apart: 4, of which 3 were waited for; matrix products, arithmetic and copies ran while one was open for 12% of the time, Pallas kernels for 0%

commit v1 on v0

v1 whole, which is shorter than its diff:
```python
import functools

import jax
import jax.numpy as jnp
from jax import lax
from jax.experimental import pallas as pl
from jax.experimental.pallas import tpu as pltpu
from jax.sharding import PartitionSpec as P

MESH = pl.DeviceIdType.MESH
F32, BF16 = jnp.float32, jnp.bfloat16
NY, NZ, NP = 4, 8, 8
CAP = 24
T = 128
D = 2048
FF = 512
CT = 512
MiB = 2**20

FAR, OWN, L1, R1, L2, R2, L3, R3 = range(8)
SRC_DIST = (4, 0, 1, 7, 2, 6, 3, 5)
CHUNKS = (
    (16, 0, OWN, 1),
    (48, 128, L1, 2),
    (48, 512, L2, 2),
    (48, 896, L3, 2),
    (32, 1280, FAR, 2),
)
SLOT_ROWS = NP * 192
PEERS = [(dy, dc) for dy in range(NY) for dc in range(2) if (dy, dc) != (0, 0)]


def place_of():
    ep = lax.axis_index("ep")
    return ep // (2 * NZ), lax.rem(ep // 2, NZ), lax.rem(ep, 2)


def device(y, z, c):
    return (y * NZ + z) * 2 + c


def remote(src, dst, send, recv, target):
    return pltpu.make_async_remote_copy(
        src, dst, send, recv, device_id={"ep": target}, device_id_type=MESH
    )


def silu(v):
    return v * (1.0 / (1.0 + jnp.exp(-v)))


def chunk_keys(meta, chunk):
    if chunk == 0:
        return meta[OWN, 0:8, :]
    if chunk == 4:
        own = meta[OWN, 0:8, :]
        own = jnp.where(own >= 16.0, own + 8.0, -1000.0)
        return jnp.concatenate([meta[FAR, 0:8, :], own], axis=1)
    first = CHUNKS[chunk][2]
    return jnp.concatenate([meta[first, 0:8, :], meta[first + 1, 0:8, :] + 24.0], axis=1)


def chunk_shares(meta, chunk):
    first, blocks = CHUNKS[chunk][2:]
    if blocks == 1:
        return meta[first, 8:16, :]
    return jnp.concatenate([meta[first, 8:16, :], meta[first + 1, 8:16, :]], axis=1)


def chunk_matches(meta, chunk):
    rows = CHUNKS[chunk][0]
    keys = chunk_keys(meta, chunk)
    number = lax.broadcasted_iota(jnp.int32, (rows, keys.shape[1]), 0).astype(F32)
    return [keys[p : p + 1, :] == number for p in range(NP)]


def moe_kernel(
    tokens,
    routes_t,
    share_t,
    norm_gain,
    switch_w,
    post_gain,
    w_gate,
    w_up,
    w_down,
    s_gate,
    s_up,
    s_down,
    mix_out,
    post_out,
    xs,
    meta_src,
    meta,
    g,
    r,
    o,
    v,
    hid,
    own,
    rs_send,
    rs_recv,
    wg,
    wu,
    wd,
    sg,
    su,
    sd,
    w_sem,
    ag_send,
    ag_recv,
    meta_send,
    meta_recv,
    y_send,
    y_recv,
    b_send,
    b_recv,
    loc_sem,
    rs_s,
    rs_r,
):
    y, z, c = place_of()
    me = y * 2 + c
    barrier = pltpu.get_barrier_semaphore()
    right = device(y, lax.rem(z + 1, NZ), c)
    left = device(y, lax.rem(z + NZ - 1, NZ), c)

    def peer(dy, dc):
        return lax.rem(y + dy, NY), lax.rem(c + dc, 2)

    for d in range(1, NZ):
        pl.semaphore_signal(
            barrier, 1, device_id={"ep": device(y, lax.rem(z + d, NZ), c)}, device_id_type=MESH
        )
    for dy, dc in PEERS:
        py, pc = peer(dy, dc)
        pl.semaphore_signal(barrier, 1, device_id={"ep": device(py, z, pc)}, device_id_type=MESH)

    loads = [
        pltpu.make_async_copy(a, b, w_sem.at[i])
        for i, (a, b) in enumerate(
            ((s_gate, sg), (s_up, su), (s_down, sd), (w_gate, wg), (w_up, wu), (w_down, wd))
        )
    ]
    for load in loads:
        load.start()

    own_rows = pl.ds(OWN * T, T)
    x = tokens[...].astype(F32)
    scale = lax.rsqrt(jnp.mean(x * x, axis=-1, keepdims=True) + 1e-06)
    xs[own_rows, :] = (x * scale * norm_gain[...]).astype(BF16)

    pl.semaphore_wait(barrier, NZ - 1 + len(PEERS))

    def block(place, first=0, rows=T):
        return xs.at[pl.ds(place * T + first, rows), :]

    def gather_step(i, src, dst, target):
        copy = remote(src, dst, ag_send.at[i], ag_recv.at[i], target)
        copy.start()
        return copy

    ag = [
        gather_step(0, block(OWN), block(L1), right),
        gather_step(1, block(OWN), block(R1), left),
    ]

    row = lax.broadcasted_iota(jnp.int32, (64, T), 0)
    in_col = lax.rem(row, 8)
    expert = (in_col // 2) * (2 * NZ) + (row // 8) * 2 + lax.rem(in_col, 2)
    gate = share_t[...]
    share = gate / jnp.sum(gate, axis=0, keepdims=True)
    named = jnp.zeros((64, T), F32)
    weight = jnp.zeros((64, T), F32)
    for k in range(10):
        hit = routes_t[k : k + 1, :] == expert
        named = named + jnp.where(hit, 1.0, 0.0)
        weight = weight + jnp.where(hit, share[k : k + 1, :], 0.0)
    earlier = lax.broadcasted_iota(jnp.int32, (T, T), 0) < lax.broadcasted_iota(
        jnp.int32, (T, T), 1
    )
    count = jnp.dot(
        named.astype(BF16), jnp.where(earlier, 1.0, 0.0).astype(BF16), preferred_element_type=F32
    )
    slot = jnp.where(named > 0.0, count, -1000.0)
    for col in range(NZ):
        meta_src[col, 0:8, :] = slot[col * 8 : col * 8 + 8, :]
        meta_src[col, 8:16, :] = weight[col * 8 : col * 8 + 8, :]
    meta[OWN] = meta_src[z]
    metas = {}
    for place, d in enumerate(SRC_DIST):
        if d:
            col = lax.rem(z + d, NZ)
            metas[place] = remote(
                meta_src.at[col], meta.at[place], meta_send.at[place], meta_recv.at[place],
                device(y, col, c),
            )
            metas[place].start()

    def peer_rows(chunk, p):
        rows, base = CHUNKS[chunk][:2]
        return pl.ds(pl.multiple_of(base + p * rows, 16), rows)

    def exchange(chunk, src, dst, send, recv, turn):
        copies = []
        for dy, dc in PEERS:
            i = dy * 2 + dc
            py, pc = peer(dy if turn > 0 else (NY - dy) % NY, dc)
            copy = remote(
                src.at[peer_rows(chunk, py * 2 + pc), :],
                dst.at[peer_rows(chunk, me), :],
                send.at[chunk, i],
                recv.at[chunk, i],
                device(py, z, pc),
            )
            copy.start()
            copies.append(copy)
        here = pltpu.make_async_copy(
            src.at[peer_rows(chunk, me), :],
            dst.at[peer_rows(chunk, me), :],
            loc_sem.at[0 if turn > 0 else 1, chunk],
        )
        here.start()
        return copies, here

    def select(chunk):
        rows, base, first, blocks = CHUNKS[chunk]
        pick = jnp.concatenate(
            [jnp.where(m, 1.0, 0.0) for m in chunk_matches(meta, chunk)], axis=0
        ).astype(BF16)

        @pl.loop(0, D // CT)
        def _(i):
            cols = pl.ds(pl.multiple_of(i * CT, CT), CT)
            g[pl.ds(base, NP * rows), cols] = jnp.dot(
                pick, xs[pl.ds(first * T, blocks * T), cols], preferred_element_type=F32
            ).astype(BF16)

        return exchange(chunk, g, r, y_send, y_recv, 1)

    def arrived(sent):
        for copy in sent[0]:
            copy.wait_recv()
        sent[1].wait()

    def run_expert(chunk):
        rows, base = CHUNKS[chunk][:2]
        n = NP * rows
        some = pl.ds(base, n)

        @pl.loop(0, FF // 256)
        def _(i):
            cols = pl.ds(pl.multiple_of(i * 256, 256), 256)
            gate_act = jnp.dot(r[some, :], wg[:, cols], preferred_element_type=F32)
            up_act = jnp.dot(r[some, :], wu[:, cols], preferred_element_type=F32)
            hid[0:n, cols] = (silu(gate_act) * up_act).astype(BF16)

        @pl.loop(0, D // CT)
        def _(i):
            cols = pl.ds(pl.multiple_of(i * CT, CT), CT)
            o[some, cols] = jnp.dot(hid[0:n, :], wd[:, cols], preferred_element_type=F32).astype(
                BF16
            )

    def give_back(chunk):
        return exchange(chunk, o, v, b_send, b_recv, -1)

    def weights_of(chunk):
        shares = chunk_shares(meta, chunk)
        w = jnp.concatenate(
            [
                jnp.where(m, shares[p : p + 1, :], 0.0)
                for p, m in enumerate(chunk_matches(meta, chunk))
            ],
            axis=0,
        )
        high = w.astype(BF16)
        return high, (w - high.astype(F32)).astype(BF16)

    def weigh(chunk, w, cols):
        rows, base = CHUNKS[chunk][:2]
        vals = v[pl.ds(base, NP * rows), cols]
        dims = (((0,), (0,)), ((), ()))
        return lax.dot_general(w[0], vals, dims, preferred_element_type=F32) + lax.dot_general(
            w[1], vals, dims, preferred_element_type=F32
        )

    out = {0: select(0)}

    for load in loads[:3]:
        load.wait()
    n_own = xs[own_rows, :]
    switch_sum = jnp.sum(n_own.astype(F32) * switch_w[...].astype(F32), axis=-1, keepdims=True)
    switch = 1.0 / (1.0 + jnp.exp(-switch_sum))
    shared = (
        silu(jnp.dot(n_own, sg[...], preferred_element_type=F32))
        * jnp.dot(n_own, su[...], preferred_element_type=F32)
    ).astype(BF16)

    @pl.loop(0, D // CT)
    def _(i):
        cols = pl.ds(pl.multiple_of(i * CT, CT), CT)
        own[:, cols] = switch * jnp.dot(shared, sd[:, cols], preferred_element_type=F32)

    ag[0].wait_recv()
    ag.append(gather_step(2, block(L1), block(L2), right))
    ag[1].wait_recv()
    ag.append(gather_step(3, block(R1), block(R2), left))
    metas[L1].wait_recv()
    metas[R1].wait_recv()
    out[1] = select(1)

    ag[2].wait_recv()
    ag.append(gather_step(4, block(L2), block(L3), right))
    ag[3].wait_recv()
    ag.append(gather_step(5, block(R2), block(R3), left))
    metas[L2].wait_recv()
    metas[R2].wait_recv()
    out[2] = select(2)

    for load in loads[3:]:
        load.wait()
    arrived(out[0])
    run_expert(0)

    ag[4].wait_recv()
    ag.append(gather_step(6, block(L3, 0, 64), block(FAR, 0, 64), right))
    ag[5].wait_recv()
    ag.append(gather_step(7, block(R3, 64, 64), block(FAR, 64, 64), left))
    metas[L3].wait_recv()
    metas[R3].wait_recv()
    out[3] = select(3)

    ag[6].wait_recv()
    ag[7].wait_recv()
    metas[FAR].wait_recv()
    out[4] = select(4)

    back = {}
    for chunk in (1, 2, 3):
        arrived(out[chunk])
        run_expert(chunk)
    back[3] = give_back(3)
    arrived(out[4])
    run_expert(4)
    back[4] = give_back(4)
    back[2] = give_back(2)

    def pass_on(i, place, first, rows, target):
        some = pl.ds(place * T + first, rows)
        copy = remote(
            rs_send.at[some, :], rs_recv.at[some, :], rs_s.at[i], rs_r.at[i], target
        )
        copy.start()
        return copy

    w4 = weights_of(4)
    arrived(back[4])

    @pl.loop(0, D // CT)
    def _(i):
        cols = pl.ds(pl.multiple_of(i * CT, CT), CT)
        part = weigh(4, w4, cols)
        rs_send[pl.ds(FAR * T, T), cols] = part[0:T, :].astype(BF16)
        own[:, cols] += part[T:, :]

    rs = [pass_on(0, FAR, 0, 64, left), pass_on(1, FAR, 64, 64, right)]
    back[1] = give_back(1)

    def add_block(chunk, w, got_left, got_right):
        first = CHUNKS[chunk][2]
        got_left = pl.ds(got_left[0], got_left[1])
        got_right = pl.ds(got_right[0], got_right[1])

        @pl.loop(0, D // CT)
        def _(i):
            cols = pl.ds(pl.multiple_of(i * CT, CT), CT)
            part = weigh(chunk, w, cols)
            a = rs_recv[got_left, cols].astype(F32)
            b = rs_recv[got_right, cols].astype(F32)
            if a.shape[0] == 64:
                more = jnp.concatenate([a, jnp.zeros((T, CT), F32), b], axis=0)
            else:
                more = jnp.concatenate([a, b], axis=0)
            rs_send[pl.ds(first * T, 2 * T), cols] = (part + more).astype(BF16)

    w3 = weights_of(3)
    arrived(back[3])
    rs[0].wait_recv()
    rs[1].wait_recv()
    add_block(3, w3, (FAR * T, 64), (FAR * T + 64, 64))
    rs += [pass_on(2, L3, 0, T, left), pass_on(3, R3, 0, T, right)]
    back[0] = give_back(0)

    w2 = weights_of(2)
    arrived(back[2])
    rs[2].wait_recv()
    rs[3].wait_recv()
    add_block(2, w2, (L3 * T, T), (R3 * T, T))
    rs += [pass_on(4, L2, 0, T, left), pass_on(5, R2, 0, T, right)]

    w1 = weights_of(1)
    arrived(back[1])
    rs[4].wait_recv()
    rs[5].wait_recv()
    add_block(1, w1, (L2 * T, T), (R2 * T, T))
    rs += [pass_on(6, L1, 0, T, left), pass_on(7, R1, 0, T, right)]

    w0 = weights_of(0)
    arrived(back[0])

    @pl.loop(0, D // CT)
    def _(i):
        cols = pl.ds(pl.multiple_of(i * CT, CT), CT)
        own[:, cols] += weigh(0, w0, cols)

    rs[6].wait_recv()
    rs[7].wait_recv()
    mixture = (
        own[...]
        + rs_recv[pl.ds(L1 * T, T), :].astype(F32)
        + rs_recv[pl.ds(R1 * T, T), :].astype(F32)
    )
    mix_out[...] = mixture.astype(BF16)
    after = tokens[...].astype(F32) + mixture
    scale = lax.rsqrt(jnp.mean(after * after, axis=-1, keepdims=True) + 1e-06)
    post_out[...] = (after * scale * post_gain[...]).astype(BF16)

    for copy in ag + rs + list(metas.values()):
        copy.wait_send()
    for sent in list(out.values()) + list(back.values()):
        for copy in sent[0]:
            copy.wait_send()


def value_kernel(post, conv_w, value_w, out, vw, wide, tail, got, w_sem, send_sem, recv_sem):
    ep = lax.axis_index("ep")
    n = lax.axis_size("ep")
    barrier = pltpu.get_barrier_semaphore()
    pl.semaphore_signal(
        barrier, 1, device_id={"ep": lax.rem(ep + n - 1, n)}, device_id_type=MESH
    )
    parts = D // CT
    loads = [
        pltpu.make_async_copy(
            value_w.at[:, pl.ds(i * CT, CT)], vw.at[:, pl.ds(i * CT, CT)], w_sem.at[i]
        )
        for i in range(parts)
    ]
    for load in loads:
        load.start()
    rows = post[...]
    for i in range(parts):
        cols = pl.ds(i * CT, CT)
        loads[i].wait()
        vals = jnp.dot(rows, vw[:, cols], preferred_element_type=F32).astype(BF16)
        wide[16 : 16 + T, cols] = vals.astype(F32)
        tail[:, cols] = vals[T - 16 :, :]
    pl.semaphore_wait(barrier, 1)
    copy = remote(tail, got, send_sem, recv_sem, lax.rem(ep + 1, n))
    copy.start()
    copy.wait_recv()
    before = jnp.where(ep > 0, 1.0, 0.0)
    wide[0:16, :] = got[...].astype(F32) * before
    for i in range(parts):
        cols = pl.ds(i * CT, CT)
        total = conv_w[0:1, cols] * wide[13 : 13 + T, cols]
        for j in range(1, 4):
            total = total + conv_w[j : j + 1, cols] * wide[13 + j : 13 + j + T, cols]
        out[:, cols] = silu(total).astype(BF16)
    copy.wait_send()


def local(
    tokens,
    routes,
    gate_share,
    norm_gain,
    w_gate,
    w_up,
    w_down,
    shared_gate,
    shared_up,
    shared_down,
    shared_switch,
    post_gain,
    value_w,
    conv_w,
):
    whole_w = lax.all_gather(value_w, "ep", axis=0, tiled=True)
    routes_t = routes.T
    share_t = gate_share.T
    vmem = pl.BlockSpec(memory_space=pltpu.VMEM)
    hbm = pl.BlockSpec(memory_space=pl.ANY)
    dma = pltpu.SemaphoreType.DMA
    mix, post = pl.pallas_call(
        moe_kernel,
        out_shape=(jax.ShapeDtypeStruct((T, D), BF16), jax.ShapeDtypeStruct((T, D), BF16)),
        in_specs=[vmem] * 6 + [hbm] * 6,
        out_specs=(vmem, vmem),
        scratch_shapes=[
            pltpu.VMEM((8 * T, D), BF16),
            pltpu.VMEM((NZ, 16, T), F32),
            pltpu.VMEM((8, 16, T), F32),
            pltpu.VMEM((SLOT_ROWS, D), BF16),
            pltpu.VMEM((SLOT_ROWS, D), BF16),
            pltpu.VMEM((SLOT_ROWS, D), BF16),
            pltpu.VMEM((SLOT_ROWS, D), BF16),
            pltpu.VMEM((NP * 48, FF), BF16),
            pltpu.VMEM((T, D), F32),
            pltpu.VMEM((8 * T, D), BF16),
            pltpu.VMEM((8 * T, D), BF16),
            pltpu.VMEM((D, FF), BF16),
            pltpu.VMEM((D, FF), BF16),
            pltpu.VMEM((FF, D), BF16),
            pltpu.VMEM(shared_gate.shape, BF16),
            pltpu.VMEM(shared_up.shape, BF16),
            pltpu.VMEM(shared_down.shape, BF16),
            dma((6,)),
            dma((8,)),
            dma((8,)),
            dma((8,)),
            dma((8,)),
            dma((5, 8)),
            dma((5, 8)),
            dma((5, 8)),
            dma((5, 8)),
            dma((2, 5)),
            dma((8,)),
            dma((8,)),
        ],
        compiler_params=pltpu.CompilerParams(
            collective_id=0, has_side_effects=True, vmem_limit_bytes=58 * MiB
        ),
        cost_estimate=pl.CostEstimate(
            flops=12 * 10**9, bytes_accessed=500 * 10**6, transcendentals=0
        ),
        name="experts",
    )(
        tokens,
        routes_t,
        share_t,
        norm_gain.reshape(1, D),
        shared_switch.reshape(1, D),
        post_gain.reshape(1, D),
        w_gate.reshape(D, FF),
        w_up.reshape(D, FF),
        w_down.reshape(FF, D),
        shared_gate,
        shared_up,
        shared_down,
    )
    conv = pl.pallas_call(
        value_kernel,
        out_shape=jax.ShapeDtypeStruct((T, D), BF16),
        in_specs=[vmem, vmem, hbm],
        out_specs=vmem,
        scratch_shapes=[
            pltpu.VMEM((D, D), BF16),
            pltpu.VMEM((16 + T, D), F32),
            pltpu.VMEM((16, D), BF16),
            pltpu.VMEM((16, D), BF16),
            dma((D // CT,)),
            dma,
            dma,
        ],
        compiler_params=pltpu.CompilerParams(
            collective_id=1, has_side_effects=True, vmem_limit_bytes=40 * MiB
        ),
        name="values",
    )(post, conv_w, whole_w)
    return mix, conv


def solution(mesh):
    placed = (
        P(("dp", "ep"), None),
        P(("dp", "ep"), None),
        P(("dp", "ep"), None),
        P(),
        P("ep", None, None),
        P("ep", None, None),
        P("ep", None, None),
        P(),
        P(),
        P(),
        P(),
        P(),
        P("ep", None),
        P(),
    )
    return jax.shard_map(
        local,
        mesh=mesh,
        in_specs=placed,
        out_specs=(P(("dp", "ep"), None), P(("dp", "ep"), None)),
        check_vma=False,
    )
```

time: 483 us -> 226 us (0.47); the launches traced: 477 us -> 225 us
  waiting for transfers between devices: 305 us -> 0.7 us
  Pallas kernels: 0 us -> 203 us
  other arithmetic: 52.8 us -> 0 us
  local copies, waits for them, and re-layouts: 54 us -> 7.3 us
  matrix products: 29.2 us -> 0 us
  starting transfers between devices: 21.9 us -> 0.04 us
    all_to_all x2 -> x0, waiting for transfers between devices: 303 us -> none  [the longest x1 164 us: local(): lax.all_to_all(outgoing, 'ep', split_axis=0, concat_axis=0, tiled=True)]
    pallas_call x0 -> x2, Pallas kernels: none -> 203 us  [the longest x1 195 us: local(): pl.pallas_call(moe_kernel, out_shape=(jax.ShapeDtypeStruct((T, D), BF16),...]
    another operation x3 -> x0, other arithmetic: 32.5 us -> none
    dot_general x6 -> x0, matrix products: 29.2 us -> none  [the longest x1 11.8 us: run_experts(): jnp.einsum('secf,efd->secd', hidden, w_down, preferred_element_type=jnp.f...]
    gather x2 -> x0, local copies, waits for them, and re-layouts: 21.6 us -> none  [the longest x1 14.5 us: local(): returned.reshape(experts_all * slots, width)[target].astype(jnp.float32)]
    all_to_all x2 -> x0, starting transfers between devices: 19.2 us -> none  [the longest x1 12.3 us: local(): lax.all_to_all(outgoing, 'ep', split_axis=0, concat_axis=0, tiled=True)]
    scatter x2 -> x0, local copies, waits for them, and re-layouts: 17.9 us -> none  [the longest x1 12.6 us: local(): filled = jnp.zeros((experts_all * slots,), jnp.bfloat16).at[target].set(j...]
    reduce_sum x4 -> x0, other arithmetic: 11 us -> none  [the longest x1 9.61 us: local(): jnp.sum((picked * shares.reshape(-1)[:, None]).reshape(tok_rows, top_coun...]
  transfers between devices with their start and end apart: 4 -> 1, of which waited for: 3 -> 0; matrix products, arithmetic and copies ran while one was open for 12% -> 1% of each run, Pallas kernels for 0% -> 87%
where the time goes in v1:
time: 226 us; the launch traced here: 225 us
  Pallas kernels  203 us (90%)
  between operations  14.1 us (6%)
  local copies, waits for them, and re-layouts  7.3 us (3%)
    pallas_call x1, Pallas kernels, local(): pl.pallas_call(moe_kernel, out_shape=(jax.ShapeDtypeStruct((T, D), BF16),...  195 us
    pallas_call x1, Pallas kernels, local(): pl.pallas_call(value_kernel, out_shape=jax.ShapeDtypeStruct((T, D), BF16)...  8.11 us
    unnamed x10, local copies, waits for them, and re-layouts  6.01 us
  transfers between devices with their start and end apart: 1, of which 0 were waited for; matrix products, arithmetic and copies ran while one was open for 1% of the time, Pallas kernels for 87%

profile of v1, /device:TPU:6, one launch (start us, length us, event | category | flops | bytes accessed | tf_op | source)
XLA Modules:
  0.0 225.3 jit_solution(7651007460895256421)
XLA Ops:
  7.2 0.0 all-gather.2.cloned.1.call-start
  7.2 0.7 all-gather.2.cloned.1.call-update
  7.9 1.3 reshape.23.switch_w
  9.2 0.0 copy-start.2
  9.2 195.1 %experts.1 = (bf16[128,2048]{1,0:T(8,128)(2,1)}, bf16[128,2048]{1,0:T(8,128)(2,1)}) custom-call(bf16[128,2048]{1,0:T(8,128)(2,1)} %tokens.1, s32[10,128]{1,0:T(8,128)} %bitcast.10, f32[10,128]{1,0:T(8,128)} %bitcast.11, f32[1,2048]{1,0:T(1,128)} %bitcast.12, bf16[1,2048]{1,0:T(2,128)(2,1)} %reshape.23.switch_w, f32[1,2048]{1,0:T(1,128)} %bitcast.13, ...), custom_call_target="tpu_custom_call" | custom-call | flops 12000000000 | bytes 500000000 | tf_op jit(solution)/shard_map/experts/pallas_call | solution.py:496
  204.3 0.0 all-gather.2.cloned.1.call-done.value_w
  204.3 0.0 copy-done.2
  204.3 0.0 copy-start
  204.3 3.4 %copy-done = bf16[2048,2048]{1,0:T(8,128)(2,1)S(1)} copy-done((bf16[2048,2048]{1,0:T(8,128)(2,1)S(1)}, bf16[2048,2048]{1,0:T(8,128)(2,1)}, u32[]{:S(2)}) %copy-start) | copy-done | bytes 8388632
  207.7 0.0 copy-start.1
  207.7 1.0 copy-done.1
  208.7 0.0 copy-start.3
  208.7 8.1 %values.1 = bf16[128,2048]{1,0:T(8,128)(2,1)S(1)} custom-call(bf16[128,2048]{1,0:T(8,128)(2,1)S(1)} %copy-done.1, f32[4,2048]{1,0:T(4,128)S(1)} %copy-done.2, bf16[2048,2048]{1,0:T(8,128)(2,1)S(1)} %copy-done), custom_call_target="tpu_custom_call" | custom-call | tf_op jit(solution)/shard_map/values/pallas_call | solution.py:553
  216.8 0.0 copy-done.3
  216.9 0.8 copy.18
  217.7 0.8 copy.19
Async XLA Ops:
  7.2 197.1 %all-gather.2.cloned.1.call-start = ((), (), s32[]{:S(2)}) async-start(), calls=%async_computation | async-start | bytes 8519680 | tf_op jit(solution)/shard_map/all_gather | solution.py:490
  9.2 195.1 %copy-start.2 = (f32[4,2048]{1,0:T(4,128)S(1)}, f32[4,2048]{1,0:T(4,128)}, u32[]{:S(2)}) copy-start(f32[4,2048]{1,0:T(4,128)} %conv_w.1) | copy-start | bytes 98308
  204.3 3.4 %copy-start = (bf16[2048,2048]{1,0:T(8,128)(2,1)S(1)}, bf16[2048,2048]{1,0:T(8,128)(2,1)}, u32[]{:S(2)}) copy-start(bf16[2048,2048]{1,0:T(8,128)(2,1)} %all-gather.2.cloned.1.call-done.value_w) | copy-start | bytes 25165828
  207.7 1.0 copy-start.1
  208.7 8.1 %copy-start.3 = (bf16[128,2048]{1,0:T(8,128)(2,1)S(1)}, bf16[128,2048]{1,0:T(8,128)(2,1)}, u32[]{:S(2)}) copy-start(bf16[128,2048]{1,0:T(8,128)(2,1)} %get-tuple-element.8) | copy-start | bytes 1572868
Sparse Core Ops, SparseCore 0:
  10.8 124.7 all-gather.1

commit v2 on v1

--- a/solution.py
+++ b/solution.py
@@ -1,5 +1,3 @@
-import functools
-
 import jax
 import jax.numpy as jnp
 from jax import lax
@@ -9,7 +7,7 @@
 
 MESH = pl.DeviceIdType.MESH
 F32, BF16 = jnp.float32, jnp.bfloat16
-NY, NZ, NP = 4, 8, 8
+NX, NY, NZ, NP = 4, 4, 8, 8
 CAP = 24
 T = 128
 D = 2048
@@ -81,24 +79,24 @@
     norm_gain,
     switch_w,
     post_gain,
+    conv_w,
     w_gate,
     w_up,
     w_down,
     s_gate,
     s_up,
     s_down,
+    value_w,
     mix_out,
-    post_out,
+    conv_out,
     xs,
     meta_src,
     meta,
     g,
     r,
-    o,
     v,
     hid,
     own,
-    rs_send,
     rs_recv,
     wg,
     wu,
@@ -106,6 +104,10 @@
     sg,
     su,
     sd,
+    vw,
+    wide,
+    tail,
+    got,
     w_sem,
     ag_send,
     ag_recv,
@@ -118,7 +120,17 @@
     loc_sem,
     rs_s,
     rs_r,
+    vy_send,
+    vy_recv,
+    vz_send,
+    vz_recv,
+    vx_send,
+    vx_recv,
+    halo_send,
+    halo_recv,
 ):
+    o, rs_send = g, xs
+    x_at, ep, n_ep = lax.axis_index("dp"), lax.axis_index("ep"), 2 * NY * NZ
     y, z, c = place_of()
     me = y * 2 + c
     barrier = pltpu.get_barrier_semaphore()
@@ -135,6 +147,13 @@
     for dy, dc in PEERS:
         py, pc = peer(dy, dc)
         pl.semaphore_signal(barrier, 1, device_id={"ep": device(py, z, pc)}, device_id_type=MESH)
+    for dx in range(1, NX):
+        pl.semaphore_signal(
+            barrier, 1, device_id={"dp": lax.rem(x_at + dx, NX), "ep": ep}, device_id_type=MESH
+        )
+    pl.semaphore_signal(
+        barrier, 1, device_id={"ep": lax.rem(ep + n_ep - 1, n_ep)}, device_id_type=MESH
+    )
 
     loads = [
         pltpu.make_async_copy(a, b, w_sem.at[i])
@@ -144,13 +163,18 @@
     ]
     for load in loads:
         load.start()
+    quarter = pl.ds(pl.multiple_of(x_at * (D // NX), D // NX), D // NX)
+    value_own = pltpu.make_async_copy(
+        value_w.at[:, quarter], vw.at[y, z, c, :, quarter], w_sem.at[6]
+    )
+    value_own.start()
 
     own_rows = pl.ds(OWN * T, T)
-    x = tokens[...].astype(F32)
-    scale = lax.rsqrt(jnp.mean(x * x, axis=-1, keepdims=True) + 1e-06)
-    xs[own_rows, :] = (x * scale * norm_gain[...]).astype(BF16)
-
-    pl.semaphore_wait(barrier, NZ - 1 + len(PEERS))
+    resid = tokens[...].astype(F32)
+    scale = lax.rsqrt(jnp.mean(resid * resid, axis=-1, keepdims=True) + 1e-06)
+    xs[own_rows, :] = (resid * scale * norm_gain[...]).astype(BF16)
+
+    pl.semaphore_wait(barrier, NZ - 1 + len(PEERS) + NX - 1 + 1)
 
     def block(place, first=0, rows=T):
         return xs.at[pl.ds(place * T + first, rows), :]
@@ -245,6 +269,8 @@
 
     def run_expert(chunk):
         rows, base = CHUNKS[chunk][:2]
+        for copy in out[chunk][0]:
+            copy.wait_send()
         n = NP * rows
         some = pl.ds(base, n)
 
@@ -286,11 +312,25 @@
         )
 
     out = {0: select(0)}
+    by_y = []
+    for dy in range(1, NY):
+        by_y.append(
+            remote(
+                value_w.at[:, quarter], vw.at[y, z, c, :, quarter], vy_send.at[dy], vy_recv.at[dy],
+                device(lax.rem(y + dy, NY), z, c),
+            )
+        )
+        by_y[-1].start()
 
     for load in loads[:3]:
         load.wait()
     n_own = xs[own_rows, :]
-    switch_sum = jnp.sum(n_own.astype(F32) * switch_w[...].astype(F32), axis=-1, keepdims=True)
+    switch_sum = jnp.zeros((T, 128), F32)
+    switch_row = switch_w[...].astype(F32)
+    for i in range(D // 128):
+        part = xs[own_rows, pl.ds(i * 128, 128)].astype(F32)
+        switch_sum = switch_sum + part * switch_row[i : i + 1, :]
+    switch_sum = jnp.sum(switch_sum, axis=-1, keepdims=True)
     switch = 1.0 / (1.0 + jnp.exp(-switch_sum))
     shared = (
         silu(jnp.dot(n_own, sg[...], preferred_element_type=F32))
@@ -331,6 +371,19 @@
     metas[R3].wait_recv()
     out[3] = select(3)
 
+    value_own.wait()
+    for copy in by_y:
+        copy.wait_recv()
+    by_z = []
+    for d in range(1, NZ):
+        part = vw.at[:, z, c, :, quarter]
+        by_z.append(
+            remote(
+                part, part, vz_send.at[d], vz_recv.at[d], device(y, lax.rem(z + d, NZ), c)
+            )
+        )
+        by_z[-1].start()
+
     ag[6].wait_recv()
     ag[7].wait_recv()
     metas[FAR].wait_recv()
@@ -341,6 +394,17 @@
         arrived(out[chunk])
         run_expert(chunk)
     back[3] = give_back(3)
+    for copy in by_z:
+        copy.wait_recv()
+    by_x = []
+    for dx in range(1, NX):
+        part = vw.at[:, :, c, :, quarter]
+        copy = pltpu.make_async_remote_copy(
+            part, part, vx_send.at[dx], vx_recv.at[dx],
+            device_id={"dp": lax.rem(x_at + dx, NX), "ep": ep}, device_id_type=MESH,
+        )
+        copy.start()
+        by_x.append(copy)
     arrived(out[4])
     run_expert(4)
     back[4] = give_back(4)
@@ -356,6 +420,8 @@
 
     w4 = weights_of(4)
     arrived(back[4])
+    for copy in ag:
+        copy.wait_send()
 
     @pl.loop(0, D // CT)
     def _(i):
@@ -399,6 +465,12 @@
     add_block(2, w2, (L3 * T, T), (R3 * T, T))
     rs += [pass_on(4, L2, 0, T, left), pass_on(5, R2, 0, T, right)]
 
+    for copy in by_x:
+        copy.wait_recv()
+    part = vw.at[:, :, c, :, :]
+    by_core = remote(part, part, vx_send.at[0], vx_recv.at[0], device(y, z, 1 - c))
+    by_core.start()
+
     w1 = weights_of(1)
     arrived(back[1])
     rs[4].wait_recv()
@@ -424,51 +496,44 @@
     mix_out[...] = mixture.astype(BF16)
     after = tokens[...].astype(F32) + mixture
     scale = lax.rsqrt(jnp.mean(after * after, axis=-1, keepdims=True) + 1e-06)
-    post_out[...] = (after * scale * post_gain[...]).astype(BF16)
-
-    for copy in ag + rs + list(metas.values()):
+    xs[own_rows, :] = (after * scale * post_gain[...]).astype(BF16)
+
+    by_core.wait_recv()
+
+    def convolve(cols, first, rows):
+        total = conv_w[0:1, cols] * wide[first + 13 : first + 13 + rows, cols]
+        for j in range(1, 4):
+            total = total + conv_w[j : j + 1, cols] * wide[first + 13 + j : first + 13 + j + rows, cols]
+        conv_out[first : first + rows, cols] = silu(total).astype(BF16)
+
+    halo = []
+    for i in range(D // CT):
+        cols = pl.ds(i * CT, CT)
+        vals = jnp.dot(
+            xs[own_rows, :], vw[:, :, :, :, cols].reshape(D, CT), preferred_element_type=F32
+        ).astype(BF16)
+        tail[:, cols] = vals[T - 16 :, :]
+        halo.append(
+            remote(
+                tail.at[:, cols], got.at[:, cols], halo_send.at[i], halo_recv.at[i],
+                lax.rem(ep + 1, n_ep),
+            )
+        )
+        halo[-1].start()
+        wide[16 : 16 + T, cols] = vals.astype(F32)
+        convolve(cols, 16, T - 16)
+    before = jnp.where(ep > 0, 1.0, 0.0)
+    for i in range(D // CT):
+        cols = pl.ds(i * CT, CT)
+        halo[i].wait_recv()
+        wide[0:16, cols] = got[:, cols].astype(F32) * before
+        convolve(cols, 0, 16)
+
+    for copy in rs + list(metas.values()) + by_y + by_z + by_x + [by_core] + halo:
         copy.wait_send()
-    for sent in list(out.values()) + list(back.values()):
+    for sent in back.values():
         for copy in sent[0]:
             copy.wait_send()
-
-
-def value_kernel(post, conv_w, value_w, out, vw, wide, tail, got, w_sem, send_sem, recv_sem):
-    ep = lax.axis_index("ep")
-    n = lax.axis_size("ep")
-    barrier = pltpu.get_barrier_semaphore()
-    pl.semaphore_signal(
-        barrier, 1, device_id={"ep": lax.rem(ep + n - 1, n)}, device_id_type=MESH
-    )
-    parts = D // CT
-    loads = [
-        pltpu.make_async_copy(
-            value_w.at[:, pl.ds(i * CT, CT)], vw.at[:, pl.ds(i * CT, CT)], w_sem.at[i]
-        )
-        for i in range(parts)
-    ]
-    for load in loads:
-        load.start()
-    rows = post[...]
-    for i in range(parts):
-        cols = pl.ds(i * CT, CT)
-        loads[i].wait()
-        vals = jnp.dot(rows, vw[:, cols], preferred_element_type=F32).astype(BF16)
-        wide[16 : 16 + T, cols] = vals.astype(F32)
-        tail[:, cols] = vals[T - 16 :, :]
-    pl.semaphore_wait(barrier, 1)
-    copy = remote(tail, got, send_sem, recv_sem, lax.rem(ep + 1, n))
-    copy.start()
-    copy.wait_recv()
-    before = jnp.where(ep > 0, 1.0, 0.0)
-    wide[0:16, :] = got[...].astype(F32) * before
-    for i in range(parts):
-        cols = pl.ds(i * CT, CT)
-        total = conv_w[0:1, cols] * wide[13 : 13 + T, cols]
-        for j in range(1, 4):
-            total = total + conv_w[j : j + 1, cols] * wide[13 + j : 13 + j + T, cols]
-        out[:, cols] = silu(total).astype(BF16)
-    copy.wait_send()
 
 
 def local(
@@ -487,16 +552,15 @@
     value_w,
     conv_w,
 ):
-    whole_w = lax.all_gather(value_w, "ep", axis=0, tiled=True)
     routes_t = routes.T
     share_t = gate_share.T
     vmem = pl.BlockSpec(memory_space=pltpu.VMEM)
     hbm = pl.BlockSpec(memory_space=pl.ANY)
     dma = pltpu.SemaphoreType.DMA
-    mix, post = pl.pallas_call(
+    return pl.pallas_call(
         moe_kernel,
         out_shape=(jax.ShapeDtypeStruct((T, D), BF16), jax.ShapeDtypeStruct((T, D), BF16)),
-        in_specs=[vmem] * 6 + [hbm] * 6,
+        in_specs=[vmem] * 7 + [hbm] * 7,
         out_specs=(vmem, vmem),
         scratch_shapes=[
             pltpu.VMEM((8 * T, D), BF16),
@@ -505,10 +569,8 @@
             pltpu.VMEM((SLOT_ROWS, D), BF16),
             pltpu.VMEM((SLOT_ROWS, D), BF16),
             pltpu.VMEM((SLOT_ROWS, D), BF16),
-            pltpu.VMEM((SLOT_ROWS, D), BF16),
             pltpu.VMEM((NP * 48, FF), BF16),
             pltpu.VMEM((T, D), F32),
-            pltpu.VMEM((8 * T, D), BF16),
             pltpu.VMEM((8 * T, D), BF16),
             pltpu.VMEM((D, FF), BF16),
             pltpu.VMEM((D, FF), BF16),
@@ -516,7 +578,11 @@
             pltpu.VMEM(shared_gate.shape, BF16),
             pltpu.VMEM(shared_up.shape, BF16),
             pltpu.VMEM(shared_down.shape, BF16),
-            dma((6,)),
+            pltpu.VMEM((NY, NZ, 2, 32, D), BF16),
+            pltpu.VMEM((16 + T, D), F32),
+            pltpu.VMEM((16, D), BF16),
+            pltpu.VMEM((16, D), BF16),
+            dma((7,)),
             dma((8,)),
             dma((8,)),
             dma((8,)),
@@ -528,12 +594,20 @@
             dma((2, 5)),
             dma((8,)),
             dma((8,)),
+            dma((4,)),
+            dma((4,)),
+            dma((8,)),
+            dma((8,)),
+            dma((4,)),
+            dma((4,)),
+            dma((4,)),
+            dma((4,)),
         ],
         compiler_params=pltpu.CompilerParams(
-            collective_id=0, has_side_effects=True, vmem_limit_bytes=58 * MiB
+            collective_id=0, has_side_effects=True, vmem_limit_bytes=60 * MiB
         ),
         cost_estimate=pl.CostEstimate(
-            flops=12 * 10**9, bytes_accessed=500 * 10**6, transcendentals=0
+            flops=13 * 10**9, bytes_accessed=500 * 10**6, transcendentals=0
         ),
         name="experts",
     )(
@@ -541,35 +615,17 @@
         routes_t,
         share_t,
         norm_gain.reshape(1, D),
-        shared_switch.reshape(1, D),
+        shared_switch.reshape(D // 128, 128),
         post_gain.reshape(1, D),
+        conv_w,
         w_gate.reshape(D, FF),
         w_up.reshape(D, FF),
         w_down.reshape(FF, D),
         shared_gate,
         shared_up,
         shared_down,
-    )
-    conv = pl.pallas_call(
-        value_kernel,
-        out_shape=jax.ShapeDtypeStruct((T, D), BF16),
-        in_specs=[vmem, vmem, hbm],
-        out_specs=vmem,
-        scratch_shapes=[
-            pltpu.VMEM((D, D), BF16),
-            pltpu.VMEM((16 + T, D), F32),
-            pltpu.VMEM((16, D), BF16),
-            pltpu.VMEM((16, D), BF16),
-            dma((D // CT,)),
-            dma,
-            dma,
-        ],
-        compiler_params=pltpu.CompilerParams(
-            collective_id=1, has_side_effects=True, vmem_limit_bytes=40 * MiB
-        ),
-        name="values",
-    )(post, conv_w, whole_w)
-    return mix, conv
+        value_w,
+    )
 
 
 def solution(mesh):

time: 226 us -> 186 us (0.82)
  Pallas kernels: 203 us -> 180 us
  between operations: 14.1 us -> 0.64 us
  local copies, waits for them, and re-layouts: 7.3 us -> 3.76 us
    pallas_call x1, Pallas kernels: 195 us -> 180 us  [local(): pl.pallas_call(moe_kernel, out_shape=(jax.ShapeDtypeStruct((T, D), BF16),...]
    pallas_call x1 -> x0, Pallas kernels: 8.11 us -> none  [local(): pl.pallas_call(value_kernel, out_shape=jax.ShapeDtypeStruct((T, D), BF16)...]
    unnamed x10 -> x2, local copies, waits for them, and re-layouts: 6.01 us -> 3.76 us
  transfers between devices with their start and end apart: 1 -> 0, of which waited for: 0 -> 0; matrix products, arithmetic and copies ran while one was open for 1% -> 0% of each run, Pallas kernels for 87% -> 0%
where the time goes in v2:
time: 186 us; the launch traced here: 184 us
  Pallas kernels  180 us (97%)
  local copies, waits for them, and re-layouts  3.76 us (2%)
    pallas_call x1, Pallas kernels, local(): pl.pallas_call(moe_kernel, out_shape=(jax.ShapeDtypeStruct((T, D), BF16),...  180 us
    unnamed x2, local copies, waits for them, and re-layouts  3.76 us

profile of v2, /device:TPU:6, one launch (start us, length us, event | category | flops | bytes accessed | tf_op | source)
XLA Modules:
  0.0 184.0 jit_solution(2076276763292909164)
XLA Ops:
  0.6 179.6 %experts.1 = (bf16[128,2048]{1,0:T(8,128)(2,1)}, bf16[128,2048]{1,0:T(8,128)(2,1)}) custom-call(bf16[128,2048]{1,0:T(8,128)(2,1)} %tokens.1, s32[10,128]{1,0:T(8,128)} %bitcast.11, f32[10,128]{1,0:T(8,128)} %bitcast.12, f32[1,2048]{1,0:T(1,128)} %bitcast.13, bf16[16,128]{1,0:T(8,128)(2,1)} %bitcast.15, f32[1,2048]{1,0:T(1,128)} %bitcast.14, ...), custom_call_target="tpu_custom_call" | custom-call | flops 12999999488 | bytes 500000000 | tf_op jit(solution)/shard_map/experts/pallas_call | solution.py:560
  180.2 1.9 %copy.18 = bf16[128,2048]{1,0:T(8,128)(2,1)} copy(bf16[128,2048]{1,0:T(8,128)(2,1)} %get-tuple-element.4) | data formatting | bytes 1048576
  182.1 1.9 %copy.19 = bf16[128,2048]{1,0:T(8,128)(2,1)} copy(bf16[128,2048]{1,0:T(8,128)(2,1)} %get-tuple-element.5) | data formatting | bytes 1048576

commit v3 on v2

--- a/solution.py
+++ b/solution.py
@@ -13,6 +13,7 @@
 D = 2048
 FF = 512
 CT = 512
+HALF = D // 2
 MiB = 2**20
 
 FAR, OWN, L1, R1, L2, R2, L3, R3 = range(8)
@@ -25,7 +26,9 @@
     (32, 1280, FAR, 2),
 )
 SLOT_ROWS = NP * 192
-PEERS = [(dy, dc) for dy in range(NY) for dc in range(2) if (dy, dc) != (0, 0)]
+ORDER = [(0, 0), (0, 1), (1, 0), (1, 1), (3, 0), (3, 1), (2, 0), (2, 1)]
+PEERS = ORDER[1:]
+NEAR = 6
 
 
 def place_of():
@@ -105,6 +108,8 @@
     su,
     sd,
     vw,
+    wd2,
+    far_hid,
     wide,
     tail,
     got,
@@ -128,6 +133,8 @@
     vx_recv,
     halo_send,
     halo_recv,
+    d_send,
+    d_recv,
 ):
     o, rs_send = g, xs
     x_at, ep, n_ep = lax.axis_index("dp"), lax.axis_index("ep"), 2 * NY * NZ
@@ -225,25 +232,47 @@
         rows, base = CHUNKS[chunk][:2]
         return pl.ds(pl.multiple_of(base + p * rows, 16), rows)
 
-    def exchange(chunk, src, dst, send, recv, turn):
+    def order_rows(chunk, q, n=1):
+        rows, base = CHUNKS[chunk][:2]
+        return pl.ds(base + q * rows, n * rows)
+
+    def send_out(chunk):
         copies = []
-        for dy, dc in PEERS:
-            i = dy * 2 + dc
-            py, pc = peer(dy if turn > 0 else (NY - dy) % NY, dc)
-            copy = remote(
-                src.at[peer_rows(chunk, py * 2 + pc), :],
-                dst.at[peer_rows(chunk, me), :],
-                send.at[chunk, i],
-                recv.at[chunk, i],
-                device(py, z, pc),
-            )
+        for q, (dy, dc) in enumerate(ORDER):
+            py, pc = peer(dy, dc)
+            src = g.at[peer_rows(chunk, py * 2 + pc), :]
+            dst = r.at[order_rows(chunk, q), :]
+            if q:
+                copies.append(
+                    remote(src, dst, y_send.at[chunk, q], y_recv.at[chunk, q], device(py, z, pc))
+                )
+            else:
+                here = pltpu.make_async_copy(src, dst, loc_sem.at[0, chunk])
+        for copy in copies:
             copy.start()
-            copies.append(copy)
-        here = pltpu.make_async_copy(
-            src.at[peer_rows(chunk, me), :],
-            dst.at[peer_rows(chunk, me), :],
-            loc_sem.at[0 if turn > 0 else 1, chunk],
-        )
+        here.start()
+        return copies, here
+
+    def far_rows(chunk):
+        rows, base = CHUNKS[chunk][:2]
+        return pl.ds(base // NP, rows)
+
+    def give_back(chunk):
+        copies = []
+        for q, (dy, dc) in enumerate(ORDER):
+            py, pc = peer((NY - dy) % NY, dc)
+            if q < NEAR:
+                src, dst = o.at[order_rows(chunk, q), :], v.at[peer_rows(chunk, me), :]
+            else:
+                src, dst = hid.at[order_rows(chunk, q), :], far_hid.at[c, far_rows(chunk), :]
+            if q:
+                copies.append(
+                    remote(src, dst, b_send.at[chunk, q], b_recv.at[chunk, q], device(py, z, pc))
+                )
+            else:
+                here = pltpu.make_async_copy(src, dst, loc_sem.at[1, chunk])
+        for copy in copies[::-1]:
+            copy.start()
         here.start()
         return copies, here
 
@@ -260,7 +289,7 @@
                 pick, xs[pl.ds(first * T, blocks * T), cols], preferred_element_type=F32
             ).astype(BF16)
 
-        return exchange(chunk, g, r, y_send, y_recv, 1)
+        return send_out(chunk)
 
     def arrived(sent):
         for copy in sent[0]:
@@ -271,25 +300,40 @@
         rows, base = CHUNKS[chunk][:2]
         for copy in out[chunk][0]:
             copy.wait_send()
-        n = NP * rows
-        some = pl.ds(base, n)
+        some = order_rows(chunk, 0, NP)
+        near = order_rows(chunk, 0, NEAR)
 
         @pl.loop(0, FF // 256)
         def _(i):
             cols = pl.ds(pl.multiple_of(i * 256, 256), 256)
             gate_act = jnp.dot(r[some, :], wg[:, cols], preferred_element_type=F32)
             up_act = jnp.dot(r[some, :], wu[:, cols], preferred_element_type=F32)
-            hid[0:n, cols] = (silu(gate_act) * up_act).astype(BF16)
+            hid[some, cols] = (silu(gate_act) * up_act).astype(BF16)
 
         @pl.loop(0, D // CT)
         def _(i):
             cols = pl.ds(pl.multiple_of(i * CT, CT), CT)
-            o[some, cols] = jnp.dot(hid[0:n, :], wd[:, cols], preferred_element_type=F32).astype(
+            o[near, cols] = jnp.dot(hid[near, :], wd[:, cols], preferred_element_type=F32).astype(
                 BF16
             )
 
-    def give_back(chunk):
-        return exchange(chunk, o, v, b_send, b_recv, -1)
+    def returned(chunk):
+        copies, here = back[chunk]
+        for copy in copies[NEAR - 1 :]:
+            copy.wait_recv()
+        py = lax.rem(y + 2, NY)
+
+        @pl.loop(0, D // CT)
+        def _(i):
+            cols = pl.ds(pl.multiple_of(i * CT, CT), CT)
+            for e in range(2):
+                v[peer_rows(chunk, py * 2 + e), cols] = jnp.dot(
+                    far_hid[e, far_rows(chunk), :], wd2[e, :, cols], preferred_element_type=F32
+                ).astype(BF16)
+
+        for copy in copies[: NEAR - 1]:
+            copy.wait_recv()
+        here.wait()
 
     def weights_of(chunk):
         shares = chunk_shares(meta, chunk)
@@ -312,6 +356,11 @@
         )
 
     out = {0: select(0)}
+    down_y = remote(
+        w_down.at[:, quarter], wd2.at[c, :, quarter], d_send.at[0], d_recv.at[0],
+        device(lax.rem(y + 2, NY), z, c),
+    )
+    down_y.start()
     by_y = []
     for dy in range(1, NY):
         by_y.append(
@@ -358,6 +407,17 @@
     metas[R2].wait_recv()
     out[2] = select(2)
 
+    down_y.wait_recv()
+    down_x = []
+    for dx in range(1, NX):
+        part = wd2.at[c, :, quarter]
+        copy = pltpu.make_async_remote_copy(
+            part, part, d_send.at[dx], d_recv.at[dx],
+            device_id={"dp": lax.rem(x_at + dx, NX), "ep": ep}, device_id_type=MESH,
+        )
+        copy.start()
+        down_x.append(copy)
+
     for load in loads[3:]:
         load.wait()
     arrived(out[0])
@@ -393,7 +453,11 @@
     for chunk in (1, 2, 3):
         arrived(out[chunk])
         run_expert(chunk)
-    back[3] = give_back(3)
+    for copy in down_x:
+        copy.wait_recv()
+    part = wd2.at[c]
+    down_core = remote(part, part, d_send.at[4], d_recv.at[4], device(y, z, 1 - c))
+    down_core.start()
     for copy in by_z:
         copy.wait_recv()
     by_x = []
@@ -408,62 +472,72 @@
     arrived(out[4])
     run_expert(4)
     back[4] = give_back(4)
+    back[3] = give_back(3)
+
+    rs = {}
+
+    def pass_on(step, h, place, first, rows, target):
+        some, cols = pl.ds(place * T + first, rows), pl.ds(h * HALF, HALF)
+        copy = remote(
+            rs_send.at[some, cols], rs_recv.at[some, cols], rs_s.at[h, step], rs_r.at[h, step], target
+        )
+        copy.start()
+        rs[step, h] = copy
+
+    def tiles(h, body):
+        @pl.loop(h * HALF // CT, (h + 1) * HALF // CT)
+        def _(i):
+            body(pl.ds(pl.multiple_of(i * CT, CT), CT))
+
+    w4 = weights_of(4)
+    down_core.wait_recv()
+    returned(4)
     back[2] = give_back(2)
-
-    def pass_on(i, place, first, rows, target):
-        some = pl.ds(place * T + first, rows)
-        copy = remote(
-            rs_send.at[some, :], rs_recv.at[some, :], rs_s.at[i], rs_r.at[i], target
-        )
-        copy.start()
-        return copy
-
-    w4 = weights_of(4)
-    arrived(back[4])
     for copy in ag:
         copy.wait_send()
 
-    @pl.loop(0, D // CT)
-    def _(i):
-        cols = pl.ds(pl.multiple_of(i * CT, CT), CT)
+    def far_part(cols):
         part = weigh(4, w4, cols)
         rs_send[pl.ds(FAR * T, T), cols] = part[0:T, :].astype(BF16)
         own[:, cols] += part[T:, :]
 
-    rs = [pass_on(0, FAR, 0, 64, left), pass_on(1, FAR, 64, 64, right)]
-    back[1] = give_back(1)
-
-    def add_block(chunk, w, got_left, got_right):
+    for h in range(2):
+        tiles(h, far_part)
+        pass_on(0, h, FAR, 0, 64, left)
+        pass_on(1, h, FAR, 64, 64, right)
+
+    def add_block(chunk, step):
+        w = weights_of(chunk)
+        returned(chunk)
+        if chunk == 3:
+            back[1] = give_back(1)
+        if chunk == 2:
+            back[0] = give_back(0)
         first = CHUNKS[chunk][2]
-        got_left = pl.ds(got_left[0], got_left[1])
-        got_right = pl.ds(got_right[0], got_right[1])
-
-        @pl.loop(0, D // CT)
-        def _(i):
-            cols = pl.ds(pl.multiple_of(i * CT, CT), CT)
+        if chunk == 3:
+            got_left, got_right = pl.ds(FAR * T, 64), pl.ds(FAR * T + 64, 64)
+        else:
+            got_left, got_right = pl.ds((first + 2) * T, T), pl.ds((first + 3) * T, T)
+
+        def add(cols):
             part = weigh(chunk, w, cols)
             a = rs_recv[got_left, cols].astype(F32)
             b = rs_recv[got_right, cols].astype(F32)
-            if a.shape[0] == 64:
+            if chunk == 3:
                 more = jnp.concatenate([a, jnp.zeros((T, CT), F32), b], axis=0)
             else:
                 more = jnp.concatenate([a, b], axis=0)
             rs_send[pl.ds(first * T, 2 * T), cols] = (part + more).astype(BF16)
 
-    w3 = weights_of(3)
-    arrived(back[3])
-    rs[0].wait_recv()
-    rs[1].wait_recv()
-    add_block(3, w3, (FAR * T, 64), (FAR * T + 64, 64))
-    rs += [pass_on(2, L3, 0, T, left), pass_on(3, R3, 0, T, right)]
-    back[0] = give_back(0)
-
-    w2 = weights_of(2)
-    arrived(back[2])
-    rs[2].wait_recv()
-    rs[3].wait_recv()
-    add_block(2, w2, (L3 * T, T), (R3 * T, T))
-    rs += [pass_on(4, L2, 0, T, left), pass_on(5, R2, 0, T, right)]
+        for h in range(2):
+            rs[step - 2, h].wait_recv()
+            rs[step - 1, h].wait_recv()
+            tiles(h, add)
+            pass_on(step, h, first, 0, T, left)
+            pass_on(step + 1, h, first + 1, 0, T, right)
+
+    add_block(3, 2)
+    add_block(2, 4)
 
     for copy in by_x:
         copy.wait_recv()
@@ -471,23 +545,19 @@
     by_core = remote(part, part, vx_send.at[0], vx_recv.at[0], device(y, z, 1 - c))
     by_core.start()
 
-    w1 = weights_of(1)
-    arrived(back[1])
-    rs[4].wait_recv()
-    rs[5].wait_recv()
-    add_block(1, w1, (L2 * T, T), (R2 * T, T))
-    rs += [pass_on(6, L1, 0, T, left), pass_on(7, R1, 0, T, right)]
+    add_block(1, 6)
 
     w0 = weights_of(0)
-    arrived(back[0])
+    returned(0)
 
     @pl.loop(0, D // CT)
     def _(i):
         cols = pl.ds(pl.multiple_of(i * CT, CT), CT)
         own[:, cols] += weigh(0, w0, cols)
 
-    rs[6].wait_recv()
-    rs[7].wait_recv()
+    for h in range(2):
+        rs[6, h].wait_recv()
+        rs[7, h].wait_recv()
     mixture = (
         own[...]
         + rs_recv[pl.ds(L1 * T, T), :].astype(F32)
@@ -529,7 +599,7 @@
         wide[0:16, cols] = got[:, cols].astype(F32) * before
         convolve(cols, 0, 16)
 
-    for copy in rs + list(metas.values()) + by_y + by_z + by_x + [by_core] + halo:
+    for copy in list(rs.values()) + list(metas.values()) + by_y + by_z + by_x + [by_core] + halo + [down_y] + down_x + [down_core]:
         copy.wait_send()
     for sent in back.values():
         for copy in sent[0]:
@@ -569,7 +639,7 @@
             pltpu.VMEM((SLOT_ROWS, D), BF16),
             pltpu.VMEM((SLOT_ROWS, D), BF16),
             pltpu.VMEM((SLOT_ROWS, D), BF16),
-            pltpu.VMEM((NP * 48, FF), BF16),
+            pltpu.VMEM((SLOT_ROWS, FF), BF16),
             pltpu.VMEM((T, D), F32),
             pltpu.VMEM((8 * T, D), BF16),
             pltpu.VMEM((D, FF), BF16),
@@ -579,6 +649,8 @@
             pltpu.VMEM(shared_up.shape, BF16),
             pltpu.VMEM(shared_down.shape, BF16),
             pltpu.VMEM((NY, NZ, 2, 32, D), BF16),
+            pltpu.VMEM((2, FF, D), BF16),
+            pltpu.VMEM((2, NP * CAP, FF), BF16),
             pltpu.VMEM((16 + T, D), F32),
             pltpu.VMEM((16, D), BF16),
             pltpu.VMEM((16, D), BF16),
@@ -592,8 +664,8 @@
             dma((5, 8)),
             dma((5, 8)),
             dma((2, 5)),
-            dma((8,)),
-            dma((8,)),
+            dma((2, 8)),
+            dma((2, 8)),
             dma((4,)),
             dma((4,)),
             dma((8,)),
@@ -602,6 +674,8 @@
             dma((4,)),
             dma((4,)),
             dma((4,)),
+            dma((5,)),
+            dma((5,)),
         ],
         compiler_params=pltpu.CompilerParams(
             collective_id=0, has_side_effects=True, vmem_limit_bytes=60 * MiB

time: 186 us -> 168 us (0.903); the launches traced: 184 us -> 168 us
  Pallas kernels: 180 us -> 164 us
    pallas_call x1, Pallas kernels: 180 us -> 164 us  [local(): pl.pallas_call(moe_kernel, out_shape=(jax.ShapeDtypeStruct((T, D), BF16),...]
where the time goes in v3:
time: 168 us
  Pallas kernels  164 us (98%)
  local copies, waits for them, and re-layouts  3.76 us (2%)
    pallas_call x1, Pallas kernels, local(): pl.pallas_call(moe_kernel, out_shape=(jax.ShapeDtypeStruct((T, D), BF16),...  164 us
    unnamed x2, local copies, waits for them, and re-layouts  3.76 us

profile of v3, /device:TPU:6, one launch (start us, length us, event | category | flops | bytes accessed | tf_op | source)
XLA Modules:
  0.0 168.1 jit_solution(9191308867861095387)
XLA Ops:
  0.6 163.7 %experts.1 = (bf16[128,2048]{1,0:T(8,128)(2,1)}, bf16[128,2048]{1,0:T(8,128)(2,1)}) custom-call(bf16[128,2048]{1,0:T(8,128)(2,1)} %tokens.1, s32[10,128]{1,0:T(8,128)} %bitcast.11, f32[10,128]{1,0:T(8,128)} %bitcast.12, f32[1,2048]{1,0:T(1,128)} %bitcast.13, bf16[16,128]{1,0:T(8,128)(2,1)} %bitcast.15, f32[1,2048]{1,0:T(1,128)} %bitcast.14, ...), custom_call_target="tpu_custom_call" | custom-call | flops 12999999488 | bytes 500000000 | tf_op jit(solution)/shard_map/experts/pallas_call | solution.py:630
  164.3 1.9 %copy.18 = bf16[128,2048]{1,0:T(8,128)(2,1)} copy(bf16[128,2048]{1,0:T(8,128)(2,1)} %get-tuple-element.4) | data formatting | bytes 1048576
  166.2 1.9 %copy.19 = bf16[128,2048]{1,0:T(8,128)(2,1)} copy(bf16[128,2048]{1,0:T(8,128)(2,1)} %get-tuple-element.5) | data formatting | bytes 1048576

commit v4 on v3

--- a/solution.py
+++ b/solution.py
@@ -429,7 +429,6 @@
     ag.append(gather_step(7, block(R3, 64, 64), block(FAR, 64, 64), left))
     metas[L3].wait_recv()
     metas[R3].wait_recv()
-    out[3] = select(3)
 
     value_own.wait()
     for copy in by_y:
@@ -448,9 +447,10 @@
     ag[7].wait_recv()
     metas[FAR].wait_recv()
     out[4] = select(4)
+    out[3] = select(3)
 
     back = {}
-    for chunk in (1, 2, 3):
+    for chunk in (1, 2):
         arrived(out[chunk])
         run_expert(chunk)
     for copy in down_x:
@@ -472,6 +472,8 @@
     arrived(out[4])
     run_expert(4)
     back[4] = give_back(4)
+    arrived(out[3])
+    run_expert(3)
     back[3] = give_back(3)
 
     rs = {}
@@ -537,14 +539,14 @@
             pass_on(step + 1, h, first + 1, 0, T, right)
 
     add_block(3, 2)
-    add_block(2, 4)
-
     for copy in by_x:
         copy.wait_recv()
     part = vw.at[:, :, c, :, :]
     by_core = remote(part, part, vx_send.at[0], vx_recv.at[0], device(y, z, 1 - c))
     by_core.start()
 
+    add_block(2, 4)
+
     add_block(1, 6)
 
     w0 = weights_of(0)
@@ -555,18 +557,22 @@
         cols = pl.ds(pl.multiple_of(i * CT, CT), CT)
         own[:, cols] += weigh(0, w0, cols)
 
+    squares = jnp.zeros((T, 1), F32)
     for h in range(2):
         rs[6, h].wait_recv()
         rs[7, h].wait_recv()
-    mixture = (
-        own[...]
-        + rs_recv[pl.ds(L1 * T, T), :].astype(F32)
-        + rs_recv[pl.ds(R1 * T, T), :].astype(F32)
-    )
-    mix_out[...] = mixture.astype(BF16)
-    after = tokens[...].astype(F32) + mixture
-    scale = lax.rsqrt(jnp.mean(after * after, axis=-1, keepdims=True) + 1e-06)
-    xs[own_rows, :] = (after * scale * post_gain[...]).astype(BF16)
+        cols = pl.ds(h * HALF, HALF)
+        mixture = (
+            own[:, cols]
+            + rs_recv[pl.ds(L1 * T, T), cols].astype(F32)
+            + rs_recv[pl.ds(R1 * T, T), cols].astype(F32)
+        )
+        mix_out[:, cols] = mixture.astype(BF16)
+        after = tokens[:, cols].astype(F32) + mixture
+        own[:, cols] = after
+        squares = squares + jnp.sum(after * after, axis=-1, keepdims=True)
+    scale = lax.rsqrt(squares * (1.0 / D) + 1e-06)
+    xs[own_rows, :] = (own[...] * scale * post_gain[...]).astype(BF16)
 
     by_core.wait_recv()
 
@@ -604,6 +610,11 @@
     for sent in back.values():
         for copy in sent[0]:
             copy.wait_send()
+
+
+def hand_on(mix, conv, mix_out, conv_out):
+    mix_out[...] = mix[...]
+    conv_out[...] = conv[...]
 
 
 def local(
@@ -627,7 +638,7 @@
     vmem = pl.BlockSpec(memory_space=pltpu.VMEM)
     hbm = pl.BlockSpec(memory_space=pl.ANY)
     dma = pltpu.SemaphoreType.DMA
-    return pl.pallas_call(
+    mix, conv = pl.pallas_call(
         moe_kernel,
         out_shape=(jax.ShapeDtypeStruct((T, D), BF16), jax.ShapeDtypeStruct((T, D), BF16)),
         in_specs=[vmem] * 7 + [hbm] * 7,
@@ -700,6 +711,13 @@
         shared_down,
         value_w,
     )
+    return pl.pallas_call(
+        hand_on,
+        out_shape=(jax.ShapeDtypeStruct((T, D), BF16), jax.ShapeDtypeStruct((T, D), BF16)),
+        in_specs=[vmem, vmem],
+        out_specs=(vmem, vmem),
+        name="outputs",
+    )(mix, conv)
 
 
 def solution(mesh):

time: 168 us -> 162 us (0.964)
  local copies, waits for them, and re-layouts: 3.76 us -> 0 us
  Pallas kernels: 164 us -> 161 us
    pallas_call x1, Pallas kernels: 164 us -> 159 us  [local(): pl.pallas_call(moe_kernel, out_shape=(jax.ShapeDtypeStruct((T, D), BF16),...]
    unnamed x2 -> x0, local copies, waits for them, and re-layouts: 3.76 us -> none
    pallas_call x0 -> x1, Pallas kernels: none -> 2.2 us  [local(): pl.pallas_call(hand_on, out_shape=(jax.ShapeDtypeStruct((T, D), BF16), ja...]
where the time goes in v4:
time: 162 us
  Pallas kernels  161 us (99%)
    pallas_call x1, Pallas kernels, local(): pl.pallas_call(moe_kernel, out_shape=(jax.ShapeDtypeStruct((T, D), BF16),...  159 us

profile of v4, /device:TPU:6, one launch (start us, length us, event | category | flops | bytes accessed | tf_op | source)
XLA Modules:
  0.0 161.6 jit_solution(9316079031042376999)
XLA Ops:
  0.6 158.8 %experts.1 = (bf16[128,2048]{1,0:T(8,128)(2,1)}, bf16[128,2048]{1,0:T(8,128)(2,1)}) custom-call(bf16[128,2048]{1,0:T(8,128)(2,1)} %tokens.1, s32[10,128]{1,0:T(8,128)} %bitcast.11, f32[10,128]{1,0:T(8,128)} %bitcast.12, f32[1,2048]{1,0:T(1,128)} %bitcast.13, bf16[16,128]{1,0:T(8,128)(2,1)} %bitcast.15, f32[1,2048]{1,0:T(1,128)} %bitcast.14, ...), custom_call_target="tpu_custom_call" | custom-call | flops 12999999488 | bytes 500000000 | tf_op jit(solution)/shard_map/experts/pallas_call | solution.py:641
  159.4 2.2 %outputs.1 = (bf16[128,2048]{1,0:T(8,128)(2,1)}, bf16[128,2048]{1,0:T(8,128)(2,1)}) custom-call(bf16[128,2048]{1,0:T(8,128)(2,1)} %get-tuple-element.4.mix, bf16[128,2048]{1,0:T(8,128)(2,1)} %get-tuple-element.5.conv), custom_call_target="tpu_custom_call" | custom-call | tf_op jit(solution)/shard_map/outputs/pallas_call | solution.py:714
